TPU v7x, 128 devices: a whole 4x4x4 slice. The times are simulated.
128 devices in a mesh: col: 4 (over x), row: 32 (over z, y, core).
Axes of the slice: x: 4, y: 4, z: 4, core: 2. Of those that a mesh axis runs over, the one named last changes fastest.
Arguments:
- velocity: bfloat16 [4, 2097152], P(None, ('col', 'row')), may hold values from -6 to 6
- pair_struct: int32 [16384], P(('col', 'row')), may hold values from 0 to 63
- pair_panel: int32 [16384], P(('col', 'row')), may hold values from 0 to 127
- pair_count: int32 [128], P(('col', 'row')), may hold values from 32 to 128, as said below
- mortar_coef: bfloat16 [16384, 128, 128], P(('col', 'row')), may hold values from -0.0625 to 0.0625
- bem_matrix: bfloat16 [32768, 32768], P('row', 'col'), may hold values from -0.03125 to 0.03125
- self_term: float32 [32768], P('row'), may hold values from 0.5 to 2
Outputs:
- pressure: bfloat16 [4, 32768], P(None, 'row')
- load: float32 [4, 2097152], P(None, ('col', 'row'))
Inputs may be any that keep to these rules, and one draw needn't show every extreme that they name: pair_struct numbers a structural block within the slot's own device. `pair_count`: some device has all its slots live.
All inputs are finite; a program needn't handle non-finite values.
Results may differ from a plain program's by a relative error of at most 0.005.
Values may be sent and summed in bfloat16 or wider, within the bound.
A program may use at most 128 MiB of HBM per device.

v0:
```python
import jax
import jax.numpy as jnp
from jax import lax
from jax.sharding import PartitionSpec as P

PANELS = 16384


def split_parts(blocks):
    return jnp.stack([blocks[..., 0::2], blocks[..., 1::2]], axis=1)


def on_device(velocity, pair_struct, pair_panel, pair_count, mortar_coef, bem_matrix, self_term):
    cases = velocity.shape[0]
    slots = pair_struct.shape[0]
    block = mortar_coef.shape[1]
    node_blocks = velocity.shape[1] // (2 * block)
    panel_blocks = PANELS // block
    live_mask = jnp.arange(slots, dtype=jnp.int32) < pair_count[0]
    vel_blocks = velocity.reshape(cases, node_blocks, 2 * block)
    picked = split_parts(jnp.take(vel_blocks, pair_struct, axis=1))
    pair_terms = jnp.einsum(
        "qpn,ckqn->ckqp", mortar_coef, picked, preferred_element_type=jnp.float32
    )
    panel_onehot = (
        (pair_panel[:, None] == jnp.arange(panel_blocks, dtype=jnp.int32)[None, :])
        & live_mask[:, None]
    ).astype(jnp.float32)
    spread_parts = jnp.einsum(
        "qb,ckqp->ckbp", panel_onehot, pair_terms, precision=lax.Precision.HIGHEST
    )
    spread_sum = spread_parts.transpose(0, 2, 3, 1).reshape(cases, 2 * PANELS)
    width_col = 2 * PANELS // lax.axis_size("col")
    width_row = 2 * PANELS // lax.axis_size("row")
    whole_sum = lax.psum(spread_sum, ("col", "row"))
    columns = lax.dynamic_slice_in_dim(
        whole_sum, lax.axis_index("col") * width_col, width_col, 1
    ).astype(jnp.bfloat16)
    row_start = lax.axis_index("row") * width_row
    owner = row_start // width_col == lax.axis_index("col")
    own_part = lax.dynamic_slice_in_dim(columns, row_start % width_col, width_row, 1).astype(
        jnp.float32
    )
    partial_value = lax.dot_general(
        columns, bem_matrix, (((1,), (1,)), ((), ())), preferred_element_type=jnp.float32
    )
    partial_value = partial_value + jnp.where(owner, self_term[None, :] * own_part, 0.0)
    pressure = lax.psum(partial_value, "col").astype(jnp.bfloat16)
    full_pressure = lax.all_gather(pressure, "row", axis=1, tiled=True)
    panel_view = full_pressure.reshape(cases, panel_blocks, 2 * block)
    took = split_parts(jnp.take(panel_view, pair_panel, axis=1))
    back_terms = jnp.einsum("qpn,ckqp->ckqn", mortar_coef, took, preferred_element_type=jnp.float32)
    node_onehot = (
        (pair_struct[:, None] == jnp.arange(node_blocks, dtype=jnp.int32)[None, :])
        & live_mask[:, None]
    ).astype(jnp.float32)
    load_parts = jnp.einsum(
        "qs,ckqn->cksn", node_onehot, back_terms, precision=lax.Precision.HIGHEST
    )
    load = load_parts.transpose(0, 2, 3, 1).reshape(cases, 2 * node_blocks * block)
    return (pressure, load)


def solution(mesh):
    placed = (
        P(None, ("col", "row")),
        P(("col", "row")),
        P(("col", "row")),
        P(("col", "row")),
        P(("col", "row"), None, None),
        P("row", "col"),
        P("row"),
    )
    return jax.shard_map(
        on_device,
        mesh=mesh,
        in_specs=placed,
        out_specs=(P(None, "row"), P(None, ("col", "row"))),
        check_vma=False,
    )
```

profile of v0, /device:TPU:1, one launch (start us, length us, event | category | flops | bytes accessed | tf_op | source)
XLA Modules:
  0.0 192.9 jit_solution(9301260147521574070)
XLA Ops:
  0.6 0.0 copy-start
  0.6 0.0 copy-start.3
  0.7 0.9 copy-done
  1.5 0.7 compare_select_fusion.1
  2.2 0.8 gather_fusion
  3.0 0.7 compare_and_fusion.1
  3.7 0.2 select_bitcast_fusion.1
  3.9 5.7 %slice.13 = bf16[4,128,128]{2,0,1:T(4,128)(2,1)S(1)} slice(bf16[4,128,256]{2,0,1:T(4,128)(2,1)S(1)} %select_bitcast_fusion.1), slice={[0:4:1], [0:128:1], [1:256:2]} | slice | bytes 262144 | tf_op jit(solution)/shard_map/slice | solution.py:10
  9.7 5.7 %slice.12 = bf16[4,128,128]{2,0,1:T(4,128)(2,1)S(1)} slice(bf16[4,128,256]{2,0,1:T(4,128)(2,1)S(1)} %select_bitcast_fusion.1), slice={[0:4:1], [0:128:1], [0:256:2]} | slice | bytes 262144 | tf_op jit(solution)/shard_map/slice | solution.py:10
  15.4 4.4 %fusion.2 = f32[128,4,2,128]{3,1,2,0:T(4,128)S(1)} fusion(bf16[128,128,128]{2,1,0:T(8,128)(2,1)} %param.11, bf16[4,1,128,128]{3,0,2,1:T(4,128)(2,1)S(1)} %bitcast.47, bf16[4,1,128,128]{3,0,2,1:T(4,128)(2,1)S(1)} %bitcast.48), kind=kOutput, calls=%fused_computation.4 | convolution fusion | flops 33685504 | bytes 4980736 | tf_op jit(solution)/shard_map/qpn,ckqn->ckqp/dot_general | solution.py:22
  19.8 0.3 copy.16
  20.8 0.0 copy-done.3
  20.8 0.4 convolution_bitcast_fusion
  21.2 12.1 %copy.9 = f32[4,128,128,2]{0,3,2,1:T(2,128)} copy(f32[4,128,128,2]{1,2,3,0:T(8,128)S(1)} %convolution_bitcast_fusion) | data formatting | bytes 1048576 | tf_op jit(solution)/shard_map/transpose;qb,ckqp->ckbp/transpose | solution.py:32
  33.4 0.0 copy-start.2
  33.4 9.5 %copy.10 = f32[4,32768]{1,0:T(4,128)S(1)} copy(f32[4,32768]{0,1:T(8,128)} %bitcast.44) | data formatting | bytes 1048576 | tf_op jit(solution)/shard_map/reshape | solution.py:32
  42.8 72.0 %all-reduce.1 = bf16[4,32768]{1,0:T(4,128)(2,1)S(1)} all-reduce(f32[4,32768]{1,0:T(4,128)S(1)} %copy.10), channel_id=1, replica_groups=mesh['col'=4,'row'=32] {'col','row'}, use_global_device_ids=true, to_apply=%region_0.1 | all-reduce | flops 131072 | bytes 786432 | tf_op jit(solution)/shard_map/psum | solution.py:35
  114.9 0.0 copy-done.2
  114.9 10.2 %convolution_add_fusion = f32[4,1024]{1,0:T(4,128)S(1)} fusion(bf16[4,8192]{1,0:T(4,128)(2,1)S(1)} %dynamic-slice_convert_fusion, bf16[1024,8192]{1,0:T(8,128)(2,1)} %param.12, s32[]{:T(128)S(6)} %select_n.48, f32[1024]{0:T(1024)S(1)} %copy-done.2, pred[]{:T(512)S(6)} %eq.34), kind=kOutput, calls=%fused_computation.8 | convolution fusion | flops 67125248 | bytes 16871428 | tf_op jit(solution)/shard_map/dot_general | solution.py:44
  125.1 0.0 copy-start.4
  125.1 13.6 %psum.15 = bf16[4,1024]{1,0:T(4,128)(2,1)S(1)} all-reduce(f32[4,1024]{1,0:T(4,128)S(1)} %convolution_add_fusion), channel_id=1, replica_groups=mesh['col'=4,'row'=32] {'col'}, use_global_device_ids=true, to_apply=%region_1.2 | all-reduce | flops 4096 | bytes 24576 | tf_op jit(solution)/shard_map/psum | solution.py:48
  138.7 0.0 copy-start.1
  138.7 26.0 %all_gather.3 = bf16[4,32768]{1,0:T(4,128)(2,1)S(1)} all-gather(bf16[4,1024]{1,0:T(4,128)(2,1)S(1)} %psum.15), channel_id=1, replica_groups=mesh['col'=4,'row'=32] {'row'}, dimensions={1}, use_global_device_ids=true | all-gather | bytes 270336 | tf_op jit(solution)/shard_map/all_gather | solution.py:49
  164.7 0.8 gather_fusion.1
  165.6 0.2 select_bitcast_fusion
  165.8 5.7 %slice.15 = bf16[4,128,128]{2,0,1:T(4,128)(2,1)S(1)} slice(bf16[4,128,256]{2,0,1:T(4,128)(2,1)S(1)} %select_bitcast_fusion), slice={[0:4:1], [0:128:1], [1:256:2]} | slice | bytes 262144 | tf_op jit(solution)/shard_map/slice | solution.py:10
  171.5 5.7 %slice.14 = bf16[4,128,128]{2,0,1:T(4,128)(2,1)S(1)} slice(bf16[4,128,256]{2,0,1:T(4,128)(2,1)S(1)} %select_bitcast_fusion), slice={[0:4:1], [0:128:1], [0:256:2]} | slice | bytes 262144 | tf_op jit(solution)/shard_map/slice | solution.py:10
  177.3 3.4 %fusion = f32[128,4,2,128]{3,1,2,0:T(4,128)S(1)} fusion(bf16[128,128,128]{2,1,0:T(8,128)(2,1)} %param.11, bf16[4,1,128,128]{3,0,2,1:T(4,128)(2,1)S(1)} %bitcast.49, bf16[4,1,128,128]{3,0,2,1:T(4,128)(2,1)S(1)} %bitcast.50), kind=kOutput, calls=%fused_computation.2 | convolution fusion | flops 33685504 | bytes 4980736 | tf_op jit(solution)/shard_map/qpn,ckqp->ckqn/dot_general | solution.py:52
  180.7 0.0 copy-done.4
  180.7 0.4 convolution_bitcast_fusion.1
  181.1 5.9 %copy.12 = f32[4,64,128,2]{0,3,2,1:T(2,128)} copy(f32[4,64,128,2]{2,1,3,0:T(8,128)S(1)} %convolution_bitcast_fusion.1) | data formatting | bytes 524288 | tf_op jit(solution)/shard_map/transpose;qs,ckqn->cksn/transpose | solution.py:60
  187.0 0.0 copy-done.1
  187.0 5.9 %copy.13 = f32[4,16384]{1,0:T(4,128)} copy(f32[4,16384]{0,1:T(8,128)} %bitcast.45) | data formatting | bytes 524288
  (6 shorter events, 0.1 us)
Async XLA Ops:
  0.6 0.9 copy-start
  0.6 20.1 %copy-start.3 = (s32[128]{0:T(128)S(1)}, s32[128]{0:T(128)}, u32[]{:S(2)}) copy-start(s32[128]{0:T(128)} %param.9) | copy-start | bytes 1540
  33.4 81.6 %copy-start.2 = (f32[1024]{0:T(1024)S(1)}, f32[1024]{0:T(1024)}, u32[]{:S(2)}) copy-start(f32[1024]{0:T(1024)} %param.13) | copy-start | bytes 12292
  125.1 55.5 %copy-start.4 = (s32[128]{0:T(128)S(1)}, s32[128]{0:T(128)}, u32[]{:S(2)}) copy-start(s32[128]{0:T(128)} %param.8) | copy-start | bytes 1540
  138.7 48.2 %copy-start.1 = (bf16[4,1024]{1,0:T(4,128)(2,1)}, bf16[4,1024]{1,0:T(4,128)(2,1)S(1)}, u32[]{:S(2)}) copy-start(bf16[4,1024]{1,0:T(4,128)(2,1)S(1)} %psum.15) | copy-start | bytes 24580
where the time goes:
time: 193 us
  blocking collectives  112 us (58%)
  local copies, waits for them, and re-layouts  59.1 us (31%)
  matrix products  18.9 us (10%)
    psum x1, blocking collectives, on_device(): whole_sum = lax.psum(spread_sum, ('col', 'row'))  72 us
    all_gather x1, blocking collectives, on_device(): full_pressure = lax.all_gather(pressure, 'row', axis=1, tiled=True)  26 us
    slice x4, local copies, waits for them, and re-layouts, split_parts(): return jnp.stack([blocks[..., 0::2], blocks[..., 1::2]], axis=1)  22.9 us
    psum x1, blocking collectives, on_device(): pressure = lax.psum(partial_value, 'col').astype(jnp.bfloat16)  13.6 us
    transpose x1, local copies, waits for them, and re-layouts, on_device(): spread_sum = spread_parts.transpose(0, 2, 3, 1).reshape(cases, 2 * PANELS)  12.1 us
    dot_general x1, matrix products, on_device(): lax.dot_general(columns, bem_matrix, (((1,), (1,)), ((), ())), preferred_...  10.2 us
    reshape x1, local copies, waits for them, and re-layouts, on_device(): spread_sum = spread_parts.transpose(0, 2, 3, 1).reshape(cases, 2 * PANELS)  9.48 us
    unnamed x11, local copies, waits for them, and re-layouts  6.83 us

commit v1 on v0

v1 whole, which is shorter than its diff:
```python
import functools

import jax
import jax.numpy as jnp
from jax import lax
from jax.experimental import pallas as pl
from jax.experimental.pallas import tpu as pltpu
from jax.sharding import PartitionSpec as P

NT = (((1,), (1,)), ((), ()))
NN = (((1,), (0,)), ((), ()))
MESH = pl.DeviceIdType.MESH
F32 = jnp.float32
BF16 = jnp.bfloat16
ROWS = 8
PER = 16
GIB = 1 << 30


def parting(width):
    src = lax.broadcasted_iota(jnp.int32, (width, width), 0)
    dst = lax.broadcasted_iota(jnp.int32, (width, width), 1)
    half = width // 2
    to = jnp.where(src % 2 == 1, half, 0) + src // 2
    return jnp.where(to == dst, 1.0, 0.0).astype(BF16)


def first_part(shape):
    return lax.broadcasted_iota(jnp.int32, shape, 0) % ROWS < ROWS // 2


def to_parts(rows, part):
    half = part.shape[0] // 2
    both = lax.dot_general(rows, part, NN, preferred_element_type=F32)
    keep = first_part((rows.shape[0], half))
    return jnp.where(keep, both[:, :half], both[:, half:])


def from_parts(rows, part):
    keep = first_part(rows.shape)
    zero = jnp.zeros_like(rows)
    wide = jnp.concatenate([jnp.where(keep, rows, zero), jnp.where(keep, zero, rows)], 1)
    return lax.dot_general(wide.astype(BF16), part, NT, preferred_element_type=F32)


def pair_products(source, take_ids, add_ids, count, coef_any, coef, sems, table, acc, dims):
    slots = coef.shape[0]
    chunks = slots // PER
    copies = [
        pltpu.make_async_copy(
            coef_any.at[pl.ds(i * PER, PER)], coef.at[pl.ds(i * PER, PER)], sems.at[i]
        )
        for i in range(chunks)
    ]
    for copy in copies:
        copy.start()
    source(table)
    acc[...] = jnp.zeros_like(acc)
    live = count[0]
    along = 1 if dims is NT else 0
    for i in range(chunks):
        copies[i].wait()

        def two(s, carry, i=i):
            q = i * PER + 2 * s
            a, b = table[take_ids[q]], table[take_ids[q + 1]]
            zero = jnp.zeros_like(a)
            left = jnp.concatenate(
                [jnp.concatenate([a, zero], 1), jnp.concatenate([zero, b], 1)], 0
            ).astype(BF16)
            right = jnp.concatenate([coef[q], coef[q + 1]], along)
            term = lax.dot_general(left, right, dims, preferred_element_type=F32)
            for k in range(2):
                where = add_ids[q + k]
                acc[where] = acc[where] + jnp.where(q + k < live, term[k * ROWS : (k + 1) * ROWS], 0.0)
            return carry

        lax.fori_loop(0, PER // 2, two, 0, unroll=PER // 2)


def forward_kernel(struct, panel, count, vel, coef_any, out, coef, sems, wide, table, acc):
    def source(table):
        vals = vel[...].astype(F32)
        both = jnp.concatenate([vals, vals], 0)
        blocks, _, width = wide.shape
        for b in range(blocks):
            wide[b] = both[:, b * width : (b + 1) * width]
        rows = wide[...].reshape(blocks * ROWS, width).astype(BF16)
        table[...] = to_parts(rows, parting(width)).reshape(table.shape)

    pair_products(source, struct, panel, count, coef_any, coef, sems, table, acc, NT)
    out[...] = acc[...].reshape(out.shape).astype(BF16)


def backward_kernel(struct, panel, count, press, coef_any, out, coef, sems, table, acc):
    def source(table):
        table[...] = press[...].astype(F32).reshape(table.shape)

    pair_products(source, panel, struct, count, coef_any, coef, sems, table, acc, NN)
    blocks, _, half = acc.shape
    part = parting(2 * half)
    rows = acc[...].reshape(blocks * ROWS, half)
    high = rows.astype(BF16).astype(F32)
    mixed = from_parts(high, part) + from_parts(rows - high, part)
    mixed = mixed.reshape(blocks, ROWS, 2 * half)
    cases = out.shape[0]
    for b in range(blocks):
        one = mixed[b]
        out[:, b * 2 * half : (b + 1) * 2 * half] = one[:cases] + one[cases:]


def field_kernel(
    nx, nz, nw, partial, bem_any, self_term, press, full,
    bem, got_x, sum_x, got_z, sum_z, got_w, mine, line, entries, terms,
    bem_sems, send, recv,
):
    col = lax.axis_index("col")
    row = lax.axis_index("row")
    z, w = row // nw, row % nw
    width = bem.shape[2] // nw
    half = width // 2
    own = press.shape[1] // width
    cases = press.shape[0]

    loads = [
        pltpu.make_async_copy(
            bem_any.at[:, pl.ds(i * nw * width, nw * width)], bem.at[i], bem_sems.at[i]
        )
        for i in range(nz)
    ]
    for load in loads:
        load.start()

    def along_x(d):
        return (lax.rem(col + d, nx), row)

    def along_z(d):
        return (col, lax.rem(z + d, nz) * nw + w)

    def along_w(d):
        return (col, z * nw + lax.rem(w + d, nw))

    xs, zs, ws = range(1, nx), range(1, nz), range(1, nw)
    friends = [along_x(d) for d in xs] + [along_z(d) for d in zs] + [along_w(d) for d in ws]
    barrier = pltpu.get_barrier_semaphore()
    for friend in friends:
        pl.semaphore_signal(barrier, inc=1, device_id=friend, device_id_type=MESH)
    pl.semaphore_wait(barrier, len(friends))

    started = []

    def go(src, dst, device):
        i = len(started)
        copy = pltpu.make_async_remote_copy(
            src_ref=src, dst_ref=dst, send_sem=send.at[i], recv_sem=recv.at[i],
            device_id=device, device_id_type=MESH,
        )
        copy.start()
        started.append(copy)
        return copy

    def rows_of(index, count):
        return pl.ds(pl.multiple_of(index * count, count), count)

    n_x = sum_x.shape[0]
    copies = [
        go(partial.at[rows_of(lax.rem(col + d, nx), n_x)], got_x.at[d - 1], along_x(d)) for d in xs
    ]
    total = partial[rows_of(col, n_x), :].astype(F32)
    for d in xs:
        copies[d - 1].wait_recv()
        total = total + got_x[d - 1].astype(F32)
    sum_x[...] = total

    n_z = sum_z.shape[0]
    copies = [
        go(sum_x.at[rows_of(lax.rem(z + d, nz), n_z)], got_z.at[d - 1], along_z(d)) for d in zs
    ]
    total = sum_x[rows_of(z, n_z), :]
    for d in zs:
        copies[d - 1].wait_recv()
        total = total + got_z[d - 1]
    sum_z[...] = total

    copies = [
        go(sum_z.at[rows_of(lax.rem(w + d, nw), ROWS)], got_w.at[d - 1], along_w(d)) for d in ws
    ]
    total = sum_z[rows_of(w, ROWS), :]
    for d in ws:
        copies[d - 1].wait_recv()
        total = total + got_w[d - 1]
    mine[rows_of(w, ROWS), :] = total.astype(BF16).astype(F32)

    copies = [go(mine.at[rows_of(w, ROWS)], mine.at[rows_of(w, ROWS)], along_w(d)) for d in ws]
    for copy in copies:
        copy.wait_recv()
    line[z] = mine[...].astype(BF16)
    copies = [go(line.at[z], line.at[z], along_z(d)) for d in zs]
    for load in loads:
        load.wait()
    part = parting(width)
    sums = jnp.zeros((ROWS, press.shape[1]), F32)
    for d in [0, *zs]:
        if d:
            copies[d - 1].wait_recv()
        at = lax.rem(z + nz - d, nz)
        lhs = from_parts(line[at].astype(F32), part)
        entries[pl.ds(at * nw, nw)] = lhs.reshape(nw, ROWS, width)
        lhs = lhs.astype(BF16)
        long = jnp.concatenate([lhs[j * ROWS : (j + 1) * ROWS] for j in range(nw)], 1)
        sums = sums + lax.dot_general(long, bem[at], NT, preferred_element_type=F32)
    first = row * own
    blocks = nz * nw
    owner = first // blocks == col
    here = lax.rem(first, blocks)
    same = jnp.concatenate([entries[here + u] for u in range(own)], 1)
    sums = sums + jnp.where(owner, same * self_term[...], 0.0)
    terms[col] = sums[:cases] + sums[cases:]

    copies = [go(terms.at[col], terms.at[col], along_x(d)) for d in xs]
    for copy in copies:
        copy.wait_recv()
    total = terms[0]
    for j in range(1, nx):
        total = total + terms[j]
    rounded = total.astype(BF16)
    press[...] = rounded
    wide = rounded.astype(F32)
    wide = jnp.concatenate([wide, wide], 0)
    wide = jnp.concatenate([wide[:, u * width : (u + 1) * width] for u in range(own)], 0)
    n_own = own * ROWS
    full[rows_of(row, n_own), :] = to_parts(wide.astype(BF16), part).astype(BF16)

    copies = [go(full.at[rows_of(row, n_own)], full.at[rows_of(row, n_own)], along_w(d)) for d in ws]
    for copy in copies:
        copy.wait_recv()
    n_line = n_own * nw
    copies = [go(full.at[rows_of(z, n_line)], full.at[rows_of(z, n_line)], along_z(d)) for d in zs]
    for copy in copies:
        copy.wait_recv()
    for copy in started:
        copy.wait_send()


def on_device(nx, nz, nw, velocity, pair_struct, pair_panel, pair_count, mortar_coef, bem_matrix, self_term):
    cases = velocity.shape[0]
    slots, panel_size, node_size = mortar_coef.shape
    node_blocks = velocity.shape[1] // (2 * node_size)
    width = 2 * panel_size
    col_blocks = bem_matrix.shape[1] // width
    panel_blocks = nx * col_blocks
    press_rows = bem_matrix.shape[0]
    own = press_rows // width
    smem = pl.BlockSpec(memory_space=pltpu.SMEM)
    vmem = pl.BlockSpec(memory_space=pltpu.VMEM)
    hbm = pl.BlockSpec(memory_space=pl.ANY)
    mortar_cost = pl.CostEstimate(
        flops=2 * ROWS * mortar_coef.size, bytes_accessed=2 * mortar_coef.size, transcendentals=0
    )
    coef_scratch = [
        pltpu.VMEM(mortar_coef.shape, BF16),
        pltpu.SemaphoreType.DMA((slots // PER,)),
    ]
    partial = pl.pallas_call(
        forward_kernel,
        out_shape=jax.ShapeDtypeStruct((panel_blocks * ROWS, panel_size), BF16),
        in_specs=[smem, smem, smem, vmem, hbm],
        out_specs=vmem,
        scratch_shapes=coef_scratch
        + [
            pltpu.VMEM((node_blocks, ROWS, 2 * node_size), F32),
            pltpu.VMEM((node_blocks, ROWS, node_size), F32),
            pltpu.VMEM((panel_blocks, ROWS, panel_size), F32),
        ],
        compiler_params=pltpu.CompilerParams(vmem_limit_bytes=24 << 20),
        cost_estimate=mortar_cost,
        name="mortar_forward",
    )(pair_struct, pair_panel, pair_count, velocity, mortar_coef)

    sends = 2 * (nx - 1) + 3 * (nz - 1) + 3 * (nw - 1)
    pressure, full = pl.pallas_call(
        functools.partial(field_kernel, nx, nz, nw),
        out_shape=(
            jax.ShapeDtypeStruct((cases, press_rows), BF16),
            jax.ShapeDtypeStruct((panel_blocks * ROWS, panel_size), BF16),
        ),
        in_specs=[vmem, hbm, vmem],
        out_specs=(vmem, vmem),
        scratch_shapes=[
            pltpu.VMEM((nz, press_rows, nw * width), BF16),
            pltpu.VMEM((nx - 1, col_blocks * ROWS, panel_size), BF16),
            pltpu.VMEM((col_blocks * ROWS, panel_size), F32),
            pltpu.VMEM((nz - 1, nw * ROWS, panel_size), F32),
            pltpu.VMEM((nw * ROWS, panel_size), F32),
            pltpu.VMEM((nw - 1, ROWS, panel_size), F32),
            pltpu.VMEM((nw * ROWS, panel_size), F32),
            pltpu.VMEM((nz, nw * ROWS, panel_size), BF16),
            pltpu.VMEM((nz * nw, ROWS, width), F32),
            pltpu.VMEM((nx, cases, press_rows), F32),
            pltpu.SemaphoreType.DMA((nz,)),
            pltpu.SemaphoreType.DMA((sends,)),
            pltpu.SemaphoreType.DMA((sends,)),
        ],
        compiler_params=pltpu.CompilerParams(
            collective_id=0, has_side_effects=True, vmem_limit_bytes=48 << 20
        ),
        cost_estimate=pl.CostEstimate(
            flops=2 * cases * bem_matrix.size,
            bytes_accessed=2 * bem_matrix.size,
            transcendentals=0,
        ),
        name="field",
    )(partial, bem_matrix, self_term[None, :])

    load = pl.pallas_call(
        backward_kernel,
        out_shape=jax.ShapeDtypeStruct(velocity.shape, F32),
        in_specs=[smem, smem, smem, vmem, hbm],
        out_specs=vmem,
        scratch_shapes=coef_scratch
        + [
            pltpu.VMEM((panel_blocks, ROWS, panel_size), F32),
            pltpu.VMEM((node_blocks, ROWS, node_size), F32),
        ],
        compiler_params=pltpu.CompilerParams(vmem_limit_bytes=24 << 20),
        cost_estimate=mortar_cost,
        name="mortar_backward",
    )(pair_struct, pair_panel, pair_count, full, mortar_coef)
    return pressure, load


def solution(mesh):
    nx = mesh.shape["col"]
    rows = mesh.shape["row"]
    nz = nx if rows % nx == 0 else 1
    placed = (
        P(None, ("col", "row")),
        P(("col", "row")),
        P(("col", "row")),
        P(("col", "row")),
        P(("col", "row"), None, None),
        P("row", "col"),
        P("row"),
    )
    return jax.shard_map(
        functools.partial(on_device, nx, nz, rows // nz),
        mesh=mesh,
        in_specs=placed,
        out_specs=(P(None, "row"), P(None, ("col", "row"))),
        check_vma=False,
    )
```

time: 193 us -> 58.6 us (0.30)
  blocking collectives: 112 us -> 0 us
  local copies, waits for them, and re-layouts: 59.1 us -> 5.69 us
  Pallas kernels: 0 us -> 51.4 us
  matrix products: 18.9 us -> 0 us
    psum x2 -> x0, blocking collectives: 85.6 us -> none  [the longest x1 72 us: on_device(): whole_sum = lax.psum(spread_sum, ('col', 'row'))]
    pallas_call x0 -> x3, Pallas kernels: none -> 51.4 us  [the longest x1 44.4 us: on_device(): pl.pallas_call(functools.partial(field_kernel, nx, nz, nw), out_shape=(ja...]
    all_gather x1 -> x0, blocking collectives: 26 us -> none  [on_device(): full_pressure = lax.all_gather(pressure, 'row', axis=1, tiled=True)]
    slice x4 -> x0, local copies, waits for them, and re-layouts: 22.9 us -> none  [split_parts(): return jnp.stack([blocks[..., 0::2], blocks[..., 1::2]], axis=1)]
    dot_general x5 -> x0, matrix products: 18.9 us -> none  [the longest x1 10.2 us: on_device(): lax.dot_general(columns, bem_matrix, (((1,), (1,)), ((), ())), preferred_...]
    transpose x2 -> x0, local copies, waits for them, and re-layouts: 18 us -> none  [the longest x1 12.1 us: on_device(): spread_sum = spread_parts.transpose(0, 2, 3, 1).reshape(cases, 2 * PANELS)]
    reshape x1 -> x0, local copies, waits for them, and re-layouts: 9.48 us -> none  [on_device(): spread_sum = spread_parts.transpose(0, 2, 3, 1).reshape(cases, 2 * PANELS)]
    unnamed x11 -> x17, local copies, waits for them, and re-layouts: 6.83 us -> 5.69 us
where the time goes in v1:
time: 58.6 us; the launch traced here: 58.4 us
  Pallas kernels  51.4 us (88%)
  local copies, waits for them, and re-layouts  5.69 us (10%)
  between operations  1.38 us (2%)
    pallas_call x1, Pallas kernels, on_device(): pl.pallas_call(functools.partial(field_kernel, nx, nz, nw), out_shape=(ja...  44.4 us
    unnamed x17, local copies, waits for them, and re-layouts  5.69 us
    pallas_call x1, Pallas kernels, on_device(): pl.pallas_call(backward_kernel, out_shape=jax.ShapeDtypeStruct(velocity.s...  3.55 us
    pallas_call x1, Pallas kernels, on_device(): pl.pallas_call(forward_kernel, out_shape=jax.ShapeDtypeStruct((panel_bloc...  3.37 us

profile of v1, /device:TPU:1, one launch (start us, length us, event | category | flops | bytes accessed | tf_op | source)
XLA Modules:
  0.0 58.4 jit_solution(4624946089234095719)
XLA Ops:
  0.6 0.0 copy-start.7
  0.6 0.0 copy-start.5
  1.3 0.0 copy-start
  1.3 2.2 %copy-done = bf16[128,128,128]{2,1,0:T(8,128)(2,1)S(1)} copy-done((bf16[128,128,128]{2,1,0:T(8,128)(2,1)S(1)}, bf16[128,128,128]{2,1,0:T(8,128)(2,1)}, u32[]{:S(2)}) %copy-start) | copy-done | bytes 4194328
  3.5 0.0 copy-start.2
  3.5 0.9 %copy-done.2 = bf16[4,16384]{1,0:T(4,128)(2,1)S(1)} copy-done((bf16[4,16384]{1,0:T(4,128)(2,1)S(1)}, bf16[4,16384]{1,0:T(4,128)(2,1)}, u32[]{:S(2)}) %copy-start.2) | copy-done | bytes 131096
  4.4 0.0 copy-start.4
  4.4 0.7 %copy-done.4 = s32[128]{0:T(128)S(1)} copy-done((s32[128]{0:T(128)S(1)}, s32[128]{0:T(128)}, u32[]{:S(2)}) %copy-start.4) | copy-done | bytes 536
  5.1 0.0 copy-start.6
  5.1 0.7 %copy-done.6 = s32[128]{0:T(128)S(1)} copy-done((s32[128]{0:T(128)S(1)}, s32[128]{0:T(128)}, u32[]{:S(2)}) %copy-start.6) | copy-done | bytes 536
  5.7 0.0 copy-start.1
  5.7 3.4 %mortar_forward.1.partial = bf16[1024,128]{1,0:T(8,128)(2,1)S(1)} custom-call(s32[128]{0:T(128)S(1)} %copy-done.4, s32[128]{0:T(128)S(1)} %copy-done.6, s32[1]{0:T(128)S(6)} %copy.10.count, bf16[4,16384]{1,0:T(4,128)(2,1)S(1)} %copy-done.2, bf16[128,128,128]{2,1,0:T(8,128)(2,1)S(1)} %copy-done), custom_call_target="tpu_custom_call" | custom-call | flops 33554432 | bytes 4194304 | tf_op jit(solution)/shard_map/mortar_forward/pallas_call | solution.py:264
  9.1 0.0 copy-start.3
  9.1 0.7 %copy-done.3 = f32[1024]{0:T(1024)S(1)} copy-done((f32[1024]{0:T(1024)S(1)}, f32[1024]{0:T(1024)}, u32[]{:S(2)}) %copy-start.3) | copy-done | bytes 4120
  9.8 44.4 %field.1 = (bf16[4,1024]{1,0:T(4,128)(2,1)S(1)}, bf16[1024,128]{1,0:T(8,128)(2,1)S(1)}) custom-call(bf16[1024,128]{1,0:T(8,128)(2,1)S(1)} %mortar_forward.1.partial, bf16[1024,8192]{1,0:T(8,128)(2,1)} %bem_any.1, f32[1,1024]{1,0:T(1,128)S(1)} %bitcast.1), custom_call_target="tpu_custom_call" | custom-call | flops 67108864 | bytes 16777216 | tf_op jit(solution)/shard_map/field/pallas_call | solution.py:281
  54.2 0.0 copy-done.7
  54.2 0.0 copy-done.5
  54.3 0.0 copy-done.1
  54.3 3.6 %mortar_backward.1 = f32[4,16384]{1,0:T(4,128)} custom-call(s32[128]{0:T(128)S(1)} %copy-done.5, s32[128]{0:T(128)S(1)} %copy-done.7, s32[1]{0:T(128)S(6)} %copy.10.count, bf16[1024,128]{1,0:T(8,128)(2,1)S(1)} %get-tuple-element.5.press, bf16[128,128,128]{2,1,0:T(8,128)(2,1)S(1)} %copy-done.1), custom_call_target="tpu_custom_call" | custom-call | flops 33554432 | bytes 4194304 | tf_op jit(solution)/shard_map/mortar_backward/pallas_call | solution.py:315
  57.8 0.6 %copy.11 = bf16[4,1024]{1,0:T(4,128)(2,1)} copy(bf16[4,1024]{1,0:T(4,128)(2,1)S(1)} %get-tuple-element.8) | data formatting | bytes 16384
Async XLA Ops:
  0.6 53.6 %copy-start.7 = (s32[128]{0:T(128)S(1)}, s32[128]{0:T(128)}, u32[]{:S(2)}) copy-start(s32[128]{0:T(128)} %panel.3) | copy-start | bytes 1540
  0.6 53.6 %copy-start.5 = (s32[128]{0:T(128)S(1)}, s32[128]{0:T(128)}, u32[]{:S(2)}) copy-start(s32[128]{0:T(128)} %struct.3) | copy-start | bytes 1540
  1.3 2.2 %copy-start = (bf16[128,128,128]{2,1,0:T(8,128)(2,1)S(1)}, bf16[128,128,128]{2,1,0:T(8,128)(2,1)}, u32[]{:S(2)}) copy-start(bf16[128,128,128]{2,1,0:T(8,128)(2,1)} %coef_any.3) | copy-start | bytes 12582916
  3.5 0.9 %copy-start.2 = (bf16[4,16384]{1,0:T(4,128)(2,1)S(1)}, bf16[4,16384]{1,0:T(4,128)(2,1)}, u32[]{:S(2)}) copy-start(bf16[4,16384]{1,0:T(4,128)(2,1)} %vel.1) | copy-start | bytes 393220
  4.4 0.7 %copy-start.4 = (s32[128]{0:T(128)S(1)}, s32[128]{0:T(128)}, u32[]{:S(2)}) copy-start(s32[128]{0:T(128)} %struct.3) | copy-start | bytes 1540
  5.1 0.7 %copy-start.6 = (s32[128]{0:T(128)S(1)}, s32[128]{0:T(128)}, u32[]{:S(2)}) copy-start(s32[128]{0:T(128)} %panel.3) | copy-start | bytes 1540
  5.7 48.5 %copy-start.1 = (bf16[128,128,128]{2,1,0:T(8,128)(2,1)S(1)}, bf16[128,128,128]{2,1,0:T(8,128)(2,1)}, u32[]{:S(2)}) copy-start(bf16[128,128,128]{2,1,0:T(8,128)(2,1)} %coef_any.3) | copy-start | bytes 12582916
  9.1 0.7 %copy-start.3 = (f32[1024]{0:T(1024)S(1)}, f32[1024]{0:T(1024)}, u32[]{:S(2)}) copy-start(f32[1024]{0:T(1024)} %param.13) | copy-start | bytes 12292

commit v2 on v0

v2 whole, which is shorter than its diff:
```python
import functools

import jax
import jax.numpy as jnp
from jax import lax
from jax.experimental import pallas as pl
from jax.experimental.pallas import tpu as pltpu
from jax.sharding import PartitionSpec as P

NT = (((1,), (1,)), ((), ()))
NN = (((1,), (0,)), ((), ()))
MESH = pl.DeviceIdType.MESH
F32 = jnp.float32
BF16 = jnp.bfloat16
ROWS = 8
PER = 16
CORES = 2
LAG = 6


def parting(width):
    src = lax.broadcasted_iota(jnp.int32, (width, width), 0)
    dst = lax.broadcasted_iota(jnp.int32, (width, width), 1)
    half = width // 2
    to = jnp.where(src % 2 == 1, half, 0) + src // 2
    return jnp.where(to == dst, 1.0, 0.0).astype(BF16)


def first_part(shape):
    return lax.broadcasted_iota(jnp.int32, shape, 0) % ROWS < ROWS // 2


def to_parts(rows, part):
    half = part.shape[0] // 2
    both = lax.dot_general(rows, part, NN, preferred_element_type=F32)
    keep = first_part((rows.shape[0], half))
    return jnp.where(keep, both[:, :half], both[:, half:])


def from_parts(rows, part):
    keep = first_part(rows.shape)
    zero = jnp.zeros_like(rows)
    wide = jnp.concatenate([jnp.where(keep, rows, zero), jnp.where(keep, zero, rows)], 1)
    return lax.dot_general(wide.astype(BF16), part, NT, preferred_element_type=F32)


def pair_term(table, ids, coef, q, dims):
    a, b = table[ids(q)], table[ids(q + 1)]
    zero = jnp.zeros_like(a)
    left = jnp.concatenate(
        [jnp.concatenate([a, zero], 1), jnp.concatenate([zero, b], 1)], 0
    ).astype(BF16)
    right = jnp.concatenate([coef[q], coef[q + 1]], 1 if dims is NT else 0)
    return lax.dot_general(left, right, dims, preferred_element_type=F32)


def backward_kernel(struct, panel, count, press, full, coef, out, press_out, table, acc):
    press_out[...] = press[...]
    table[...] = full[...].astype(F32).reshape(table.shape)
    acc[...] = jnp.zeros_like(acc)
    live = count[0, 0]

    def two(s, carry):
        q = 2 * s
        term = pair_term(table, lambda i: panel[0, i], coef, q, NN)
        for k in range(2):
            where = struct[0, q + k]
            acc[where] = acc[where] + jnp.where(q + k < live, term[k * ROWS : (k + 1) * ROWS], 0.0)
        return carry

    lax.fori_loop(0, coef.shape[0] // 2, two, 0, unroll=PER // 2)
    blocks, _, half = acc.shape
    part = parting(2 * half)
    rows = acc[...].reshape(blocks * ROWS, half)
    high = rows.astype(BF16).astype(F32)
    mixed = from_parts(high, part) + from_parts(rows - high, part)
    mixed = mixed.reshape(blocks, ROWS, 2 * half)
    cases = out.shape[0]
    for b in range(blocks):
        one = mixed[b]
        out[:, b * 2 * half : (b + 1) * 2 * half] = one[:cases] + one[cases:]


def field_kernel(
    nx, nz, ny, count, struct_any, panel_any, vel_any, coef_any, bem_any, self_any,
    press, full,
    struct, panel, panel_row, vel, coef, bem, self_term, wide, table, pair_rows,
    sums_all, got_core, half_16, got_zy, sum_zy, got_x, line, terms,
    in_sems, coef_sems, bem_sems, send, recv,
):
    col = lax.axis_index("col")
    row = lax.axis_index("row")
    chip, core = row // CORES, row % CORES
    z, y = chip // ny, chip % ny
    chips = nz * ny
    slots, size, _ = coef.shape
    width = 2 * size
    cases, press_rows = press.shape
    own = press_rows // width

    small = [
        (struct_any, struct), (panel_any, panel),
        (panel_any, panel_row), (vel_any, vel), (self_any, self_term),
    ]
    ins = [pltpu.make_async_copy(a, b, in_sems.at[i]) for i, (a, b) in enumerate(small)]
    coefs = [
        pltpu.make_async_copy(
            coef_any.at[pl.ds(i * PER, PER)], coef.at[pl.ds(i * PER, PER)], coef_sems.at[i]
        )
        for i in range(slots // PER)
    ]
    wide_chip = CORES * width
    loads = [
        pltpu.make_async_copy(
            bem_any.at[:, pl.ds(i * wide_chip, wide_chip)], bem.at[i], bem_sems.at[i]
        )
        for i in range(chips)
    ]
    for copy in [*ins, *coefs]:
        copy.start()

    def at_x(d):
        return (lax.rem(col + d, nx), row)

    def chip_at(dz, dy):
        return lax.rem(z + dz + nz, nz) * ny + lax.rem(y + dy + ny, ny)

    def at_zy(step):
        return (col, chip_at(*step) * CORES + core)

    def hops(step):
        return min(step[0], nz - step[0]) + min(step[1], ny - step[1])

    sibling = (col, chip * CORES + 1 - core)
    xs = range(1, nx)
    near = sorted([(a, b) for a in range(nz) for b in range(ny) if a or b], key=hops)
    friends = [at_zy(s) for s in near[::-1]] + [at_x(d) for d in xs] + [sibling]
    barrier = pltpu.get_barrier_semaphore()
    for friend in friends:
        pl.semaphore_signal(barrier, inc=1, device_id=friend, device_id_type=MESH)

    started = []

    def go(src, dst, device):
        i = len(started)
        copy = pltpu.make_async_remote_copy(
            src_ref=src, dst_ref=dst, send_sem=send.at[i], recv_sem=recv.at[i],
            device_id=device, device_id_type=MESH,
        )
        copy.start()
        started.append(copy)
        return copy

    def rows_of(index, n):
        return pl.ds(pl.multiple_of(index * n, n), n)

    part = parting(width)
    for copy in ins:
        copy.wait()
    vals = vel[...].astype(F32)
    both = jnp.concatenate([vals, vals], 0)
    node_blocks = wide.shape[0]
    for b in range(node_blocks):
        wide[b] = both[:, b * width : (b + 1) * width]
    table[...] = to_parts(
        wide[...].reshape(node_blocks * ROWS, width).astype(BF16), part
    ).reshape(table.shape)
    for i in range(slots // PER):
        coefs[i].wait()
        if i == slots // PER - 1:
            for load in loads:
                load.start()

        def two(s, carry, i=i):
            q = i * PER + 2 * s
            term = pair_term(table, lambda j: struct[0, j], coef, q, NT)
            pair_rows[pl.ds(pl.multiple_of(q * ROWS, 2 * ROWS), 2 * ROWS), :] = term
            return carry

        lax.fori_loop(0, PER // 2, two, 0, unroll=PER // 2)

    panel_blocks = nx * chips * CORES
    place = lax.broadcasted_iota(jnp.int32, (panel_blocks, slots), 0)
    block = (place % nx) * (chips * CORES) + (place // nx) % chips * CORES + place // (nx * chips)
    slot = lax.broadcasted_iota(jnp.int32, (panel_blocks, slots), 1)
    hit = (panel_row[...] == block) & (slot < count[0, 0])
    hit = jnp.where(hit, 1.0, 0.0).astype(BF16)
    hit = jnp.concatenate([hit, hit], 1)
    for r in range(ROWS):
        term = pair_rows[pl.ds(r, slots, stride=ROWS), :]
        high = term.astype(BF16)
        low = (term - high.astype(F32)).astype(BF16)
        sums_all[pl.ds(r, panel_blocks, stride=ROWS), :] = lax.dot_general(
            hit, jnp.concatenate([high, low], 0), NN, preferred_element_type=F32
        )

    pl.semaphore_wait(barrier, len(friends))

    n_core = got_core.shape[0]
    copy = go(sums_all.at[rows_of(1 - core, n_core)], got_core, sibling)
    copy.wait_recv()
    half_16[...] = (sums_all[rows_of(core, n_core), :] + got_core[...]).astype(BF16)

    n_zy = nx * ROWS
    copies = {
        s: go(half_16.at[rows_of(chip_at(*s), n_zy)], got_zy.at[k], at_zy(s))
        for k, s in reversed(list(enumerate(near)))
    }
    mine = rows_of(core * chips + chip, n_zy), rows_of(chip, n_zy)
    total = sums_all[mine[0], :] + got_core[mine[1], :]
    for k, s in enumerate(near):
        copies[s].wait_recv()
        total = total + got_zy[k].astype(F32)
    sum_zy[...] = total

    copies = [go(sum_zy.at[rows_of(lax.rem(col + d, nx), ROWS)], got_x.at[d - 1], at_x(d)) for d in xs]
    total = sum_zy[rows_of(col, ROWS), :]
    for d in xs:
        copies[d - 1].wait_recv()
        total = total + got_x[d - 1]
    mixed = from_parts(total.astype(BF16).astype(F32), part)
    line[row] = jnp.concatenate([mixed[:, :size], mixed[:, size:]], 0).astype(BF16)

    def spread(ref, done, lag):
        piece = {s: go(ref(row), ref(row), at_zy(s)) for s in near[::-1]}
        pending = [(go(ref(row), ref(row), sibling), chip)]
        done(row)

        def beside():
            copy, source = pending.pop(0)
            copy.wait_recv()
            done(source * CORES + 1 - core)

        for s in near:
            source = chip_at(-s[0], -s[1])
            piece[s].wait_recv()
            came = source * CORES + core
            pending.append((go(ref(came), ref(came), sibling), source))
            done(came)
            if len(pending) > lag:
                beside()
        while pending:
            beside()

    def entries(r):
        both = line[r].astype(F32)
        return jnp.concatenate([both[:ROWS], both[ROWS:]], 1)

    sums = [jnp.zeros((ROWS, press_rows), F32)]

    def product(r):
        of_chip = r // CORES
        at = pl.ds(pl.multiple_of(lax.rem(r, CORES) * width, width), width)
        sums[0] = sums[0] + lax.dot_general(
            entries(r).astype(BF16), bem[of_chip, :, at], NT, preferred_element_type=F32
        )

    for load in loads:
        load.wait()
    spread(lambda r: line.at[r], product, LAG)

    first = row * own
    blocks = chips * CORES
    owner = first // blocks == col
    here = lax.rem(first, blocks)
    same = jnp.concatenate([entries(here + u) for u in range(own)], 1)
    summed = sums[0] + jnp.where(owner, same * self_term[...], 0.0)
    terms[col] = summed[:cases] + summed[cases:]

    copies = [go(terms.at[col], terms.at[col], at_x(d)) for d in xs]
    for copy in copies:
        copy.wait_recv()
    total = terms[0]
    for j in range(1, nx):
        total = total + terms[j]
    rounded = total.astype(BF16)
    press[...] = rounded
    tall = rounded.astype(F32)
    tall = jnp.concatenate([tall, tall], 0)
    tall = jnp.concatenate([tall[:, u * width : (u + 1) * width] for u in range(own)], 0)
    n_own = own * ROWS
    full[rows_of(row, n_own), :] = to_parts(tall.astype(BF16), part).astype(BF16)

    spread(lambda r: full.at[rows_of(r, n_own)], lambda r: None, chips)
    for copy in started:
        copy.wait_send()


def on_device(nx, nz, ny, velocity, pair_struct, pair_panel, pair_count, mortar_coef, bem_matrix, self_term):
    cases = velocity.shape[0]
    slots, panel_size, node_size = mortar_coef.shape
    node_blocks = velocity.shape[1] // (2 * node_size)
    width = 2 * panel_size
    press_rows = bem_matrix.shape[0]
    chips = nz * ny
    col_blocks = chips * CORES
    panel_blocks = nx * col_blocks
    smem = pl.BlockSpec(memory_space=pltpu.SMEM)
    vmem = pl.BlockSpec(memory_space=pltpu.VMEM)
    hbm = pl.BlockSpec(memory_space=pltpu.HBM)
    struct, panel, count = pair_struct[None, :], pair_panel[None, :], pair_count[None, :]

    steps = chips - 1
    sends = 1 + steps + 2 * (nx - 1) + 2 * (2 * steps + 1)
    dma = pltpu.SemaphoreType.DMA
    pressure, full = pl.pallas_call(
        functools.partial(field_kernel, nx, nz, ny),
        out_shape=(
            jax.ShapeDtypeStruct((cases, press_rows), BF16),
            jax.ShapeDtypeStruct((panel_blocks * ROWS, panel_size), BF16),
        ),
        in_specs=[smem] + [hbm] * 6,
        out_specs=(vmem, vmem),
        scratch_shapes=[
            pltpu.SMEM((1, slots), jnp.int32),
            pltpu.SMEM((1, slots), jnp.int32),
            pltpu.VMEM((1, slots), jnp.int32),
            pltpu.VMEM(velocity.shape, BF16),
            pltpu.VMEM(mortar_coef.shape, BF16),
            pltpu.VMEM((chips, press_rows, CORES * width), BF16),
            pltpu.VMEM((1, press_rows), F32),
            pltpu.VMEM((node_blocks, ROWS, 2 * node_size), F32),
            pltpu.VMEM((node_blocks, ROWS, node_size), F32),
            pltpu.VMEM((slots * ROWS, panel_size), F32),
            pltpu.VMEM((panel_blocks * ROWS, panel_size), F32),
            pltpu.VMEM((panel_blocks * ROWS // CORES, panel_size), F32),
            pltpu.VMEM((panel_blocks * ROWS // CORES, panel_size), BF16),
            pltpu.VMEM((steps, nx * ROWS, panel_size), BF16),
            pltpu.VMEM((nx * ROWS, panel_size), F32),
            pltpu.VMEM((nx - 1, ROWS, panel_size), F32),
            pltpu.VMEM((col_blocks, 2 * ROWS, panel_size), BF16),
            pltpu.VMEM((nx, cases, press_rows), F32),
            dma((5,)),
            dma((slots // PER,)),
            dma((chips,)),
            dma((sends,)),
            dma((sends,)),
        ],
        compiler_params=pltpu.CompilerParams(
            collective_id=0, has_side_effects=True, vmem_limit_bytes=44 << 20
        ),
        cost_estimate=pl.CostEstimate(
            flops=2 * cases * bem_matrix.size,
            bytes_accessed=2 * bem_matrix.size,
            transcendentals=0,
        ),
        name="field",
    )(
        count,
        *[
            pltpu.with_memory_space_constraint(x, pltpu.HBM)
            for x in (struct, panel, velocity, mortar_coef, bem_matrix, self_term[None, :])
        ],
    )

    load, pressure = pl.pallas_call(
        backward_kernel,
        out_shape=(
            jax.ShapeDtypeStruct(velocity.shape, F32),
            jax.ShapeDtypeStruct((cases, press_rows), BF16),
        ),
        in_specs=[smem, smem, smem, vmem, vmem, vmem],
        out_specs=(vmem, vmem),
        scratch_shapes=[
            pltpu.VMEM((panel_blocks, ROWS, panel_size), F32),
            pltpu.VMEM((node_blocks, ROWS, node_size), F32),
        ],
        compiler_params=pltpu.CompilerParams(vmem_limit_bytes=24 << 20),
        cost_estimate=pl.CostEstimate(
            flops=2 * ROWS * mortar_coef.size,
            bytes_accessed=2 * mortar_coef.size,
            transcendentals=0,
        ),
        name="mortar_backward",
    )(struct, panel, count, pressure, full, mortar_coef)
    return pressure, load


def solution(mesh):
    nx = mesh.shape["col"]
    chips = mesh.shape["row"] // CORES
    nz = nx if chips % nx == 0 else 1
    placed = (
        P(None, ("col", "row")),
        P(("col", "row")),
        P(("col", "row")),
        P(("col", "row")),
        P(("col", "row"), None, None),
        P("row", "col"),
        P("row"),
    )
    return jax.shard_map(
        functools.partial(on_device, nx, nz, chips // nz),
        mesh=mesh,
        in_specs=placed,
        out_specs=(P(None, "row"), P(None, ("col", "row"))),
        check_vma=False,
    )
```

time: 193 us -> 47.1 us (0.24)
  blocking collectives: 112 us -> 0 us
  local copies, waits for them, and re-layouts: 59.1 us -> 0.01 us
  Pallas kernels: 0 us -> 45.5 us
  matrix products: 18.9 us -> 0 us
    psum x2 -> x0, blocking collectives: 85.6 us -> none  [the longest x1 72 us: on_device(): whole_sum = lax.psum(spread_sum, ('col', 'row'))]
    pallas_call x0 -> x2, Pallas kernels: none -> 45.5 us  [the longest x1 42.3 us: on_device(): pl.pallas_call(functools.partial(field_kernel, nx, nz, ny), out_shape=(ja...]
    all_gather x1 -> x0, blocking collectives: 26 us -> none  [on_device(): full_pressure = lax.all_gather(pressure, 'row', axis=1, tiled=True)]
    slice x4 -> x0, local copies, waits for them, and re-layouts: 22.9 us -> none  [split_parts(): return jnp.stack([blocks[..., 0::2], blocks[..., 1::2]], axis=1)]
    dot_general x5 -> x0, matrix products: 18.9 us -> none  [the longest x1 10.2 us: on_device(): lax.dot_general(columns, bem_matrix, (((1,), (1,)), ((), ())), preferred_...]
    transpose x2 -> x0, local copies, waits for them, and re-layouts: 18 us -> none  [the longest x1 12.1 us: on_device(): spread_sum = spread_parts.transpose(0, 2, 3, 1).reshape(cases, 2 * PANELS)]
    reshape x1 -> x0, local copies, waits for them, and re-layouts: 9.48 us -> none  [on_device(): spread_sum = spread_parts.transpose(0, 2, 3, 1).reshape(cases, 2 * PANELS)]
    unnamed x11 -> x6, local copies, waits for them, and re-layouts: 6.83 us -> 0.01 us
where the time goes in v2:
time: 47.1 us; the launch traced here: 47 us
  Pallas kernels  45.5 us (97%)
  between operations  1.48 us (3%)
    pallas_call x1, Pallas kernels, on_device(): pl.pallas_call(functools.partial(field_kernel, nx, nz, ny), out_shape=(ja...  42.3 us
    pallas_call x1, Pallas kernels, on_device(): pl.pallas_call(backward_kernel, out_shape=(jax.ShapeDtypeStruct(velocity....  3.27 us

profile of v2, /device:TPU:1, one launch (start us, length us, event | category | flops | bytes accessed | tf_op | source)
XLA Modules:
  0.0 47.0 jit_solution(4852091855222218713)
XLA Ops:
  0.6 0.0 copy-start
  0.6 0.0 copy-start.2
  0.7 0.0 copy-start.1
  1.5 42.3 %field.1 = (bf16[4,1024]{1,0:T(4,128)(2,1)S(1)}, bf16[1024,128]{1,0:T(8,128)(2,1)S(1)}) custom-call(s32[1,1]{1,0:T(1,128)} %bitcast.4.count, s32[1,128]{1,0:T(1,128)} %bitcast.6, s32[1,128]{1,0:T(1,128)} %bitcast.8, bf16[4,16384]{1,0:T(4,128)(2,1)} %vel_any.1, bf16[128,128,128]{2,1,0:T(8,128)(2,1)} %coef.1, bf16[1024,8192]{1,0:T(8,128)(2,1)} %bem_any.1, ...), custom_call_target="tpu_custom_call" | custom-call | flops 67108864 | bytes 16777216 | tf_op jit(solution)/shard_map/field/pallas_call | solution.py:306
  43.7 0.0 copy-done
  43.7 0.0 copy-done.2
  43.8 0.0 copy-done.1
  43.8 3.3 %mortar_backward.1 = (f32[4,16384]{1,0:T(4,128)}, bf16[4,1024]{1,0:T(4,128)(2,1)}) custom-call(s32[1,128]{1,0:T(1,128)S(1)} %bitcast.7, s32[1,128]{1,0:T(1,128)S(1)} %bitcast.9, s32[1,1]{1,0:T(1,128)} %bitcast.5.count, bf16[4,1024]{1,0:T(4,128)(2,1)S(1)} %get-tuple-element.6.press, bf16[1024,128]{1,0:T(8,128)(2,1)S(1)} %get-tuple-element.7.full, ...), custom_call_target="tpu_custom_call" | custom-call | flops 33554432 | bytes 4194304 | tf_op jit(solution)/shard_map/mortar_backward/pallas_call | solution.py:356
Async XLA Ops:
  0.6 43.1 %copy-start = (bf16[128,128,128]{2,1,0:T(8,128)(2,1)S(1)}, bf16[128,128,128]{2,1,0:T(8,128)(2,1)}, u32[]{:S(2)}) copy-start(bf16[128,128,128]{2,1,0:T(8,128)(2,1)} %coef.1) | copy-start | bytes 12582916
  0.6 43.1 %copy-start.2 = (s32[128]{0:T(128)S(1)}, s32[128]{0:T(128)}, u32[]{:S(2)}) copy-start(s32[128]{0:T(128)} %param.9) | copy-start | bytes 1540
  0.7 43.1 %copy-start.1 = (s32[128]{0:T(128)S(1)}, s32[128]{0:T(128)}, u32[]{:S(2)}) copy-start(s32[128]{0:T(128)} %param.8) | copy-start | bytes 1540

commit v3 on v2

--- a/solution.py
+++ b/solution.py
@@ -1,4 +1,5 @@
 import functools
+import itertools
 
 import jax
 import jax.numpy as jnp
@@ -15,7 +16,7 @@
 ROWS = 8
 PER = 16
 CORES = 2
-LAG = 6
+AHEAD = 3
 
 
 def parting(width):
@@ -68,7 +69,7 @@
             acc[where] = acc[where] + jnp.where(q + k < live, term[k * ROWS : (k + 1) * ROWS], 0.0)
         return carry
 
-    lax.fori_loop(0, coef.shape[0] // 2, two, 0, unroll=PER // 2)
+    lax.fori_loop(0, coef.shape[0] // 2, two, 0, unroll=min(32, coef.shape[0] // 2))
     blocks, _, half = acc.shape
     part = parting(2 * half)
     rows = acc[...].reshape(blocks * ROWS, half)
@@ -83,9 +84,9 @@
 
 def field_kernel(
     nx, nz, ny, count, struct_any, panel_any, vel_any, coef_any, bem_any, self_any,
-    press, full,
-    struct, panel, panel_row, vel, coef, bem, self_term, wide, table, pair_rows,
-    sums_all, got_core, half_16, got_zy, sum_zy, got_x, line, terms,
+    press, full, coef,
+    struct, panel, panel_row, vel, bem, self_term, wide, table, pair_rows,
+    sums_all, got_core, got_all, line, terms,
     in_sems, coef_sems, bem_sems, send, recv,
 ):
     col = lax.axis_index("col")
@@ -109,43 +110,45 @@
         )
         for i in range(slots // PER)
     ]
-    wide_chip = CORES * width
     loads = [
-        pltpu.make_async_copy(
-            bem_any.at[:, pl.ds(i * wide_chip, wide_chip)], bem.at[i], bem_sems.at[i]
-        )
-        for i in range(chips)
+        pltpu.make_async_copy(bem_any.at[:, pl.ds(i * width, width)], bem.at[i], bem_sems.at[i])
+        for i in range(chips * CORES)
     ]
-    for copy in [*ins, *coefs]:
+    for copy in [*ins, *coefs[:AHEAD]]:
         copy.start()
-
-    def at_x(d):
-        return (lax.rem(col + d, nx), row)
 
     def chip_at(dz, dy):
         return lax.rem(z + dz + nz, nz) * ny + lax.rem(y + dy + ny, ny)
 
-    def at_zy(step):
-        return (col, chip_at(*step) * CORES + core)
+    def at(step):
+        return (lax.rem(col + step[0], nx), row_at(step[1:]))
+
+    def row_at(step):
+        return chip_at(*step[:2]) * CORES + (1 - core if step[2] else core)
 
     def hops(step):
-        return min(step[0], nz - step[0]) + min(step[1], ny - step[1])
-
-    sibling = (col, chip * CORES + 1 - core)
+        return sum(min(d, n - d) for d, n in zip(step, (nx, nz, ny)))
+
+    def steps(x_range, cores):
+        every = itertools.product(x_range, range(nz), range(ny), range(cores))
+        return sorted([s for s in every if any(s)], key=lambda s: (hops(s), s))
+
+    sibling = (0, 0, 0, 1)
     xs = range(1, nx)
-    near = sorted([(a, b) for a in range(nz) for b in range(ny) if a or b], key=hops)
-    friends = [at_zy(s) for s in near[::-1]] + [at_x(d) for d in xs] + [sibling]
+    to_owner = steps(range(nx), 1)
+    in_col = steps((0,), CORES)
+    friends = sorted({*to_owner, *in_col}, key=lambda s: (-hops(s), s))
     barrier = pltpu.get_barrier_semaphore()
     for friend in friends:
-        pl.semaphore_signal(barrier, inc=1, device_id=friend, device_id_type=MESH)
+        pl.semaphore_signal(barrier, inc=1, device_id=at(friend), device_id_type=MESH)
 
     started = []
 
-    def go(src, dst, device):
+    def go(src, dst, step):
         i = len(started)
         copy = pltpu.make_async_remote_copy(
             src_ref=src, dst_ref=dst, send_sem=send.at[i], recv_sem=recv.at[i],
-            device_id=device, device_id_type=MESH,
+            device_id=at(step), device_id_type=MESH,
         )
         copy.start()
         started.append(copy)
@@ -167,7 +170,9 @@
     ).reshape(table.shape)
     for i in range(slots // PER):
         coefs[i].wait()
-        if i == slots // PER - 1:
+        for copy in coefs[i + AHEAD : i + AHEAD + 1]:
+            copy.start()
+        if i == len(coefs) - 1:
             for load in loads:
                 load.start()
 
@@ -199,75 +204,68 @@
     n_core = got_core.shape[0]
     copy = go(sums_all.at[rows_of(1 - core, n_core)], got_core, sibling)
     copy.wait_recv()
-    half_16[...] = (sums_all[rows_of(core, n_core), :] + got_core[...]).astype(BF16)
-
-    n_zy = nx * ROWS
+    got_core[...] = sums_all[rows_of(core, n_core), :] + got_core[...]
+
+    def block_at(step):
+        return rows_of(chip_at(*step[1:3]) * nx + lax.rem(col + step[0], nx), ROWS)
+
     copies = {
-        s: go(half_16.at[rows_of(chip_at(*s), n_zy)], got_zy.at[k], at_zy(s))
-        for k, s in reversed(list(enumerate(near)))
+        s: go(got_core.at[block_at(s)], got_all.at[k], s)
+        for k, s in reversed(list(enumerate(to_owner)))
     }
-    mine = rows_of(core * chips + chip, n_zy), rows_of(chip, n_zy)
-    total = sums_all[mine[0], :] + got_core[mine[1], :]
-    for k, s in enumerate(near):
+    total = got_core[block_at((0, 0, 0, 0)), :]
+    for k, s in enumerate(to_owner):
         copies[s].wait_recv()
-        total = total + got_zy[k].astype(F32)
-    sum_zy[...] = total
-
-    copies = [go(sum_zy.at[rows_of(lax.rem(col + d, nx), ROWS)], got_x.at[d - 1], at_x(d)) for d in xs]
-    total = sum_zy[rows_of(col, ROWS), :]
-    for d in xs:
-        copies[d - 1].wait_recv()
-        total = total + got_x[d - 1]
+        total = total + got_all[k]
     mixed = from_parts(total.astype(BF16).astype(F32), part)
     line[row] = jnp.concatenate([mixed[:, :size], mixed[:, size:]], 0).astype(BF16)
 
-    def spread(ref, done, lag):
-        piece = {s: go(ref(row), ref(row), at_zy(s)) for s in near[::-1]}
-        pending = [(go(ref(row), ref(row), sibling), chip)]
-        done(row)
-
-        def beside():
-            copy, source = pending.pop(0)
-            copy.wait_recv()
-            done(source * CORES + 1 - core)
-
-        for s in near:
-            source = chip_at(-s[0], -s[1])
+    def source(s):
+        return row_at((-s[1], -s[2], s[3]))
+
+    def send_out(ref, over):
+        return {s: go(ref(row), ref(row), s) for s in over[::-1]}
+
+    def came(piece, over):
+        over = list(over)
+        for s in over:
             piece[s].wait_recv()
-            came = source * CORES + core
-            pending.append((go(ref(came), ref(came), sibling), source))
-            done(came)
-            if len(pending) > lag:
-                beside()
-        while pending:
-            beside()
+        return [source(s) for s in over]
 
     def entries(r):
         both = line[r].astype(F32)
         return jnp.concatenate([both[:ROWS], both[ROWS:]], 1)
 
-    sums = [jnp.zeros((ROWS, press_rows), F32)]
-
-    def product(r):
-        of_chip = r // CORES
-        at = pl.ds(pl.multiple_of(lax.rem(r, CORES) * width, width), width)
-        sums[0] = sums[0] + lax.dot_general(
-            entries(r).astype(BF16), bem[of_chip, :, at], NT, preferred_element_type=F32
-        )
-
+    split = press_rows * 5 // 8
+
+    def products(rows):
+        still, moving = 0.0, 0.0
+        for r in rows:
+            x = entries(r).astype(BF16)
+            still += lax.dot_general(x, bem[r, :split], NT, preferred_element_type=F32)
+            moving += lax.dot_general(bem[r, split:], x, NT, preferred_element_type=F32)
+        return still, moving
+
+    def plus(one, other):
+        return one[0] + other[0], one[1] + other[1]
+
+    piece = send_out(lambda r: line.at[r], in_col)
     for load in loads:
         load.wait()
-    spread(lambda r: line.at[r], product, LAG)
+    sums = products([row])
+    for _, group in itertools.groupby(in_col, key=hops):
+        sums = plus(sums, products(came(piece, group)))
+    sums = jnp.concatenate([sums[0], sums[1].T], 1)
 
     first = row * own
     blocks = chips * CORES
     owner = first // blocks == col
     here = lax.rem(first, blocks)
     same = jnp.concatenate([entries(here + u) for u in range(own)], 1)
-    summed = sums[0] + jnp.where(owner, same * self_term[...], 0.0)
+    summed = sums + jnp.where(owner, same * self_term[...], 0.0)
     terms[col] = summed[:cases] + summed[cases:]
 
-    copies = [go(terms.at[col], terms.at[col], at_x(d)) for d in xs]
+    copies = [go(terms.at[col], terms.at[col], (d, 0, 0, 0)) for d in xs]
     for copy in copies:
         copy.wait_recv()
     total = terms[0]
@@ -281,7 +279,10 @@
     n_own = own * ROWS
     full[rows_of(row, n_own), :] = to_parts(tall.astype(BF16), part).astype(BF16)
 
-    spread(lambda r: full.at[rows_of(r, n_own)], lambda r: None, chips)
+    def full_at(r):
+        return full.at[rows_of(r, n_own)]
+
+    came(send_out(full_at, in_col), in_col)
     for copy in started:
         copy.wait_send()
 
@@ -300,39 +301,35 @@
     hbm = pl.BlockSpec(memory_space=pltpu.HBM)
     struct, panel, count = pair_struct[None, :], pair_panel[None, :], pair_count[None, :]
 
-    steps = chips - 1
-    sends = 1 + steps + 2 * (nx - 1) + 2 * (2 * steps + 1)
+    sends = nx * chips + 2 * (col_blocks - 1) + nx - 1
     dma = pltpu.SemaphoreType.DMA
-    pressure, full = pl.pallas_call(
+    pressure, full, coef = pl.pallas_call(
         functools.partial(field_kernel, nx, nz, ny),
         out_shape=(
             jax.ShapeDtypeStruct((cases, press_rows), BF16),
             jax.ShapeDtypeStruct((panel_blocks * ROWS, panel_size), BF16),
+            jax.ShapeDtypeStruct(mortar_coef.shape, BF16),
         ),
         in_specs=[smem] + [hbm] * 6,
-        out_specs=(vmem, vmem),
+        out_specs=(vmem, vmem, vmem),
         scratch_shapes=[
             pltpu.SMEM((1, slots), jnp.int32),
             pltpu.SMEM((1, slots), jnp.int32),
             pltpu.VMEM((1, slots), jnp.int32),
             pltpu.VMEM(velocity.shape, BF16),
-            pltpu.VMEM(mortar_coef.shape, BF16),
-            pltpu.VMEM((chips, press_rows, CORES * width), BF16),
+            pltpu.VMEM((col_blocks, press_rows, width), BF16),
             pltpu.VMEM((1, press_rows), F32),
             pltpu.VMEM((node_blocks, ROWS, 2 * node_size), F32),
             pltpu.VMEM((node_blocks, ROWS, node_size), F32),
             pltpu.VMEM((slots * ROWS, panel_size), F32),
             pltpu.VMEM((panel_blocks * ROWS, panel_size), F32),
             pltpu.VMEM((panel_blocks * ROWS // CORES, panel_size), F32),
-            pltpu.VMEM((panel_blocks * ROWS // CORES, panel_size), BF16),
-            pltpu.VMEM((steps, nx * ROWS, panel_size), BF16),
-            pltpu.VMEM((nx * ROWS, panel_size), F32),
-            pltpu.VMEM((nx - 1, ROWS, panel_size), F32),
+            pltpu.VMEM((nx * chips - 1, ROWS, panel_size), F32),
             pltpu.VMEM((col_blocks, 2 * ROWS, panel_size), BF16),
             pltpu.VMEM((nx, cases, press_rows), F32),
             dma((5,)),
             dma((slots // PER,)),
-            dma((chips,)),
+            dma((col_blocks,)),
             dma((sends,)),
             dma((sends,)),
         ],
@@ -372,7 +369,7 @@
             transcendentals=0,
         ),
         name="mortar_backward",
-    )(struct, panel, count, pressure, full, mortar_coef)
+    )(struct, panel, count, pressure, full, coef)
     return pressure, load
 
 

time: 47.1 us -> 41.5 us (0.88)
  Pallas kernels: 45.5 us -> 40 us
    pallas_call x1, Pallas kernels: 42.3 us -> 37.4 us  [on_device(): pl.pallas_call(functools.partial(field_kernel, nx, nz, ny), out_shape=(ja...]
    pallas_call x1, Pallas kernels: 3.27 us -> 2.55 us  [on_device(): pl.pallas_call(backward_kernel, out_shape=(jax.ShapeDtypeStruct(velocity....]
where the time goes in v3:
time: 41.5 us; the launch traced here: 41.3 us
  Pallas kernels  40 us (96%)
  between operations  1.32 us (3%)
    pallas_call x1, Pallas kernels, on_device(): pl.pallas_call(functools.partial(field_kernel, nx, nz, ny), out_shape=(ja...  37.4 us
    pallas_call x1, Pallas kernels, on_device(): pl.pallas_call(backward_kernel, out_shape=(jax.ShapeDtypeStruct(velocity....  2.55 us

profile of v3, /device:TPU:1, one launch (start us, length us, event | category | flops | bytes accessed | tf_op | source)
XLA Modules:
  0.0 41.3 jit_solution(15156879255010282738)
XLA Ops:
  1.3 0.0 copy-start
  1.3 0.0 copy-start.1
  1.3 37.4 %field.1 = (bf16[4,1024]{1,0:T(4,128)(2,1)S(1)}, bf16[1024,128]{1,0:T(8,128)(2,1)S(1)}, bf16[128,128,128]{2,1,0:T(8,128)(2,1)S(1)}) custom-call(s32[1,1]{1,0:T(1,128)} %bitcast.4.count, s32[1,128]{1,0:T(1,128)} %bitcast.6, s32[1,128]{1,0:T(1,128)} %bitcast.8, bf16[4,16384]{1,0:T(4,128)(2,1)} %vel_any.1, bf16[128,128,128]{2,1,0:T(8,128)(2,1)} %coef_any.1, ...), custom_call_target="tpu_custom_call" | custom-call | flops 67108864 | bytes 16777216 | tf_op jit(solution)/shard_map/field/pallas_call | solution.py:306
  38.7 0.0 copy-done
  38.7 0.0 copy-done.1
  38.7 2.5 %mortar_backward.1 = (f32[4,16384]{1,0:T(4,128)}, bf16[4,1024]{1,0:T(4,128)(2,1)}) custom-call(s32[1,128]{1,0:T(1,128)S(1)} %bitcast.7, s32[1,128]{1,0:T(1,128)S(1)} %bitcast.9, s32[1,1]{1,0:T(1,128)} %bitcast.5.count, bf16[4,1024]{1,0:T(4,128)(2,1)S(1)} %get-tuple-element.7.press, bf16[1024,128]{1,0:T(8,128)(2,1)S(1)} %get-tuple-element.8.full, ...), custom_call_target="tpu_custom_call" | custom-call | flops 33554432 | bytes 4194304 | tf_op jit(solution)/shard_map/mortar_backward/pallas_call | solution.py:353
Async XLA Ops:
  1.3 37.4 %copy-start = (s32[128]{0:T(128)S(1)}, s32[128]{0:T(128)}, u32[]{:S(2)}) copy-start(s32[128]{0:T(128)} %param.8) | copy-start | bytes 1540
  1.3 37.4 %copy-start.1 = (s32[128]{0:T(128)S(1)}, s32[128]{0:T(128)}, u32[]{:S(2)}) copy-start(s32[128]{0:T(128)} %param.9) | copy-start | bytes 1540

commit v4 on v3

--- a/solution.py
+++ b/solution.py
@@ -14,7 +14,7 @@
 F32 = jnp.float32
 BF16 = jnp.bfloat16
 ROWS = 8
-PER = 16
+PER = 32
 CORES = 2
 AHEAD = 3
 
@@ -86,7 +86,7 @@
     nx, nz, ny, count, struct_any, panel_any, vel_any, coef_any, bem_any, self_any,
     press, full, coef,
     struct, panel, panel_row, vel, bem, self_term, wide, table, pair_rows,
-    sums_all, got_core, got_all, line, terms,
+    other_half, own_half, got_core, got_all, line, terms,
     in_sems, coef_sems, bem_sems, send, recv,
 ):
     col = lax.axis_index("col")
@@ -137,7 +137,7 @@
     xs = range(1, nx)
     to_owner = steps(range(nx), 1)
     in_col = steps((0,), CORES)
-    friends = sorted({*to_owner, *in_col}, key=lambda s: (-hops(s), s))
+    friends = [*to_owner[::-1], sibling]
     barrier = pltpu.get_barrier_semaphore()
     for friend in friends:
         pl.semaphore_signal(barrier, inc=1, device_id=at(friend), device_id_type=MESH)
@@ -184,27 +184,32 @@
 
         lax.fori_loop(0, PER // 2, two, 0, unroll=PER // 2)
 
-    panel_blocks = nx * chips * CORES
-    place = lax.broadcasted_iota(jnp.int32, (panel_blocks, slots), 0)
-    block = (place % nx) * (chips * CORES) + (place // nx) % chips * CORES + place // (nx * chips)
-    slot = lax.broadcasted_iota(jnp.int32, (panel_blocks, slots), 1)
-    hit = (panel_row[...] == block) & (slot < count[0, 0])
-    hit = jnp.where(hit, 1.0, 0.0).astype(BF16)
-    hit = jnp.concatenate([hit, hit], 1)
+    terms_16 = []
     for r in range(ROWS):
         term = pair_rows[pl.ds(r, slots, stride=ROWS), :]
         high = term.astype(BF16)
         low = (term - high.astype(F32)).astype(BF16)
-        sums_all[pl.ds(r, panel_blocks, stride=ROWS), :] = lax.dot_general(
-            hit, jnp.concatenate([high, low], 0), NN, preferred_element_type=F32
-        )
-
+        terms_16.append(jnp.concatenate([high, low], 0))
+    half_blocks = nx * chips
+    place = lax.broadcasted_iota(jnp.int32, (half_blocks, slots), 0)
+    block = (place % nx) * (chips * CORES) + place // nx * CORES
+    slot = lax.broadcasted_iota(jnp.int32, (half_blocks, slots), 1)
+    live = slot < count[0, 0]
+
+    def block_sums(of_core, into):
+        hit = jnp.where((panel_row[...] == block + of_core) & live, 1.0, 0.0).astype(BF16)
+        hit = jnp.concatenate([hit, hit], 1)
+        for r in range(ROWS):
+            into[pl.ds(r, half_blocks, stride=ROWS), :] = lax.dot_general(
+                hit, terms_16[r], NN, preferred_element_type=F32
+            )
+
+    block_sums(1 - core, other_half)
     pl.semaphore_wait(barrier, len(friends))
-
-    n_core = got_core.shape[0]
-    copy = go(sums_all.at[rows_of(1 - core, n_core)], got_core, sibling)
+    copy = go(other_half, got_core, sibling)
+    block_sums(core, own_half)
     copy.wait_recv()
-    got_core[...] = sums_all[rows_of(core, n_core), :] + got_core[...]
+    got_core[...] = own_half[...] + got_core[...]
 
     def block_at(step):
         return rows_of(chip_at(*step[1:3]) * nx + lax.rem(col + step[0], nx), ROWS)
@@ -322,7 +327,8 @@
             pltpu.VMEM((node_blocks, ROWS, 2 * node_size), F32),
             pltpu.VMEM((node_blocks, ROWS, node_size), F32),
             pltpu.VMEM((slots * ROWS, panel_size), F32),
-            pltpu.VMEM((panel_blocks * ROWS, panel_size), F32),
+            pltpu.VMEM((panel_blocks * ROWS // CORES, panel_size), F32),
+            pltpu.VMEM((panel_blocks * ROWS // CORES, panel_size), F32),
             pltpu.VMEM((panel_blocks * ROWS // CORES, panel_size), F32),
             pltpu.VMEM((nx * chips - 1, ROWS, panel_size), F32),
             pltpu.VMEM((col_blocks, 2 * ROWS, panel_size), BF16),

time: 41.5 us -> 41.2 us (level)
  no operation moved by 1% of the time
where the time goes in v4:
time: 41.2 us; the launch traced here: 41.1 us
  Pallas kernels  39.7 us (96%)
  between operations  1.32 us (3%)
    pallas_call x1, Pallas kernels, on_device(): pl.pallas_call(functools.partial(field_kernel, nx, nz, ny), out_shape=(ja...  37.2 us
    pallas_call x1, Pallas kernels, on_device(): pl.pallas_call(backward_kernel, out_shape=(jax.ShapeDtypeStruct(velocity....  2.55 us

profile of v4, /device:TPU:1, one launch (start us, length us, event | category | flops | bytes accessed | tf_op | source)
XLA Modules:
  0.0 41.1 jit_solution(3573503562931656819)
XLA Ops:
  1.3 0.0 copy-start
  1.3 0.0 copy-start.1
  1.3 37.2 %field.1 = (bf16[4,1024]{1,0:T(4,128)(2,1)S(1)}, bf16[1024,128]{1,0:T(8,128)(2,1)S(1)}, bf16[128,128,128]{2,1,0:T(8,128)(2,1)S(1)}) custom-call(s32[1,1]{1,0:T(1,128)} %bitcast.4.count, s32[1,128]{1,0:T(1,128)} %bitcast.6, s32[1,128]{1,0:T(1,128)} %bitcast.8, bf16[4,16384]{1,0:T(4,128)(2,1)} %vel_any.1, bf16[128,128,128]{2,1,0:T(8,128)(2,1)} %coef_any.1, ...), custom_call_target="tpu_custom_call" | custom-call | flops 67108864 | bytes 16777216 | tf_op jit(solution)/shard_map/field/pallas_call | solution.py:311
  38.5 0.0 copy-done
  38.5 0.0 copy-done.1
  38.5 2.6 %mortar_backward.1 = (f32[4,16384]{1,0:T(4,128)}, bf16[4,1024]{1,0:T(4,128)(2,1)}) custom-call(s32[1,128]{1,0:T(1,128)S(1)} %bitcast.7, s32[1,128]{1,0:T(1,128)S(1)} %bitcast.9, s32[1,1]{1,0:T(1,128)} %bitcast.5.count, bf16[4,1024]{1,0:T(4,128)(2,1)S(1)} %get-tuple-element.7.press, bf16[1024,128]{1,0:T(8,128)(2,1)S(1)} %get-tuple-element.8.full, ...), custom_call_target="tpu_custom_call" | custom-call | flops 33554432 | bytes 4194304 | tf_op jit(solution)/shard_map/mortar_backward/pallas_call | solution.py:359
Async XLA Ops:
  1.3 37.2 %copy-start = (s32[128]{0:T(128)S(1)}, s32[128]{0:T(128)}, u32[]{:S(2)}) copy-start(s32[128]{0:T(128)} %param.8) | copy-start | bytes 1540
  1.3 37.2 %copy-start.1 = (s32[128]{0:T(128)S(1)}, s32[128]{0:T(128)}, u32[]{:S(2)}) copy-start(s32[128]{0:T(128)} %param.9) | copy-start | bytes 1540

commit v5 on v4

--- a/solution.py
+++ b/solution.py
@@ -14,9 +14,9 @@
 F32 = jnp.float32
 BF16 = jnp.bfloat16
 ROWS = 8
-PER = 32
+PER = 64
 CORES = 2
-AHEAD = 3
+AHEAD = 8
 
 
 def parting(width):
@@ -69,7 +69,7 @@
             acc[where] = acc[where] + jnp.where(q + k < live, term[k * ROWS : (k + 1) * ROWS], 0.0)
         return carry
 
-    lax.fori_loop(0, coef.shape[0] // 2, two, 0, unroll=min(32, coef.shape[0] // 2))
+    lax.fori_loop(0, coef.shape[0] // 2, two, 0, unroll=coef.shape[0] // 2)
     blocks, _, half = acc.shape
     part = parting(2 * half)
     rows = acc[...].reshape(blocks * ROWS, half)

time: 41.2 us -> 41 us (level)
  no operation moved by 1% of the time
where the time goes in v5:
time: 41 us; the launch traced here: 40.8 us
  Pallas kernels  39.5 us (96%)
  between operations  1.32 us (3%)
    pallas_call x1, Pallas kernels, on_device(): pl.pallas_call(functools.partial(field_kernel, nx, nz, ny), out_shape=(ja...  37.2 us
    pallas_call x1, Pallas kernels, on_device(): pl.pallas_call(backward_kernel, out_shape=(jax.ShapeDtypeStruct(velocity....  2.35 us

profile of v5, /device:TPU:1, one launch (start us, length us, event | category | flops | bytes accessed | tf_op | source)
XLA Modules:
  0.0 40.8 jit_solution(11504779947223928638)
XLA Ops:
  1.3 0.0 copy-start
  1.3 0.0 copy-start.1
  1.3 37.2 %field.1 = (bf16[4,1024]{1,0:T(4,128)(2,1)S(1)}, bf16[1024,128]{1,0:T(8,128)(2,1)S(1)}, bf16[128,128,128]{2,1,0:T(8,128)(2,1)S(1)}) custom-call(s32[1,1]{1,0:T(1,128)} %bitcast.4.count, s32[1,128]{1,0:T(1,128)} %bitcast.6, s32[1,128]{1,0:T(1,128)} %bitcast.8, bf16[4,16384]{1,0:T(4,128)(2,1)} %vel_any.1, bf16[128,128,128]{2,1,0:T(8,128)(2,1)} %coef_any.1, ...), custom_call_target="tpu_custom_call" | custom-call | flops 67108864 | bytes 16777216 | tf_op jit(solution)/shard_map/field/pallas_call | solution.py:311
  38.5 0.0 copy-done
  38.5 0.0 copy-done.1
  38.5 2.4 %mortar_backward.1 = (f32[4,16384]{1,0:T(4,128)}, bf16[4,1024]{1,0:T(4,128)(2,1)}) custom-call(s32[1,128]{1,0:T(1,128)S(1)} %bitcast.7, s32[1,128]{1,0:T(1,128)S(1)} %bitcast.9, s32[1,1]{1,0:T(1,128)} %bitcast.5.count, bf16[4,1024]{1,0:T(4,128)(2,1)S(1)} %get-tuple-element.7.press, bf16[1024,128]{1,0:T(8,128)(2,1)S(1)} %get-tuple-element.8.full, ...), custom_call_target="tpu_custom_call" | custom-call | flops 33554432 | bytes 4194304 | tf_op jit(solution)/shard_map/mortar_backward/pallas_call | solution.py:359
Async XLA Ops:
  1.3 37.2 %copy-start = (s32[128]{0:T(128)S(1)}, s32[128]{0:T(128)}, u32[]{:S(2)}) copy-start(s32[128]{0:T(128)} %param.8) | copy-start | bytes 1540
  1.3 37.2 %copy-start.1 = (s32[128]{0:T(128)S(1)}, s32[128]{0:T(128)}, u32[]{:S(2)}) copy-start(s32[128]{0:T(128)} %param.9) | copy-start | bytes 1540

commit v6 on v5

--- a/solution.py
+++ b/solution.py
@@ -258,9 +258,14 @@
     for load in loads:
         load.wait()
     sums = products([row])
-    for _, group in itertools.groupby(in_col, key=hops):
+    groups = [list(group) for _, group in itertools.groupby(in_col, key=hops)]
+    for group in groups[:-1]:
         sums = plus(sums, products(came(piece, group)))
     sums = jnp.concatenate([sums[0], sums[1].T], 1)
+    for r in came(piece, groups[-1]):
+        sums += lax.dot_general(
+            entries(r).astype(BF16), bem[r], NT, preferred_element_type=F32
+        )
 
     first = row * own
     blocks = chips * CORES

time: 41 us -> 41 us (level)
  no operation moved by 1% of the time
where the time goes in v6:
time: 41 us; the launch traced here: 40.9 us
  Pallas kernels  39.6 us (97%)
  between operations  1.32 us (3%)
    pallas_call x1, Pallas kernels, on_device(): pl.pallas_call(functools.partial(field_kernel, nx, nz, ny), out_shape=(ja...  37.2 us
    pallas_call x1, Pallas kernels, on_device(): pl.pallas_call(backward_kernel, out_shape=(jax.ShapeDtypeStruct(velocity....  2.36 us

profile of v6, /device:TPU:1, one launch (start us, length us, event | category | flops | bytes accessed | tf_op | source)
XLA Modules:
  0.0 40.9 jit_solution(10534771512802341888)
XLA Ops:
  1.3 0.0 copy-start
  1.3 0.0 copy-start.1
  1.3 37.2 %field.1 = (bf16[4,1024]{1,0:T(4,128)(2,1)S(1)}, bf16[1024,128]{1,0:T(8,128)(2,1)S(1)}, bf16[128,128,128]{2,1,0:T(8,128)(2,1)S(1)}) custom-call(s32[1,1]{1,0:T(1,128)} %bitcast.4.count, s32[1,128]{1,0:T(1,128)} %bitcast.6, s32[1,128]{1,0:T(1,128)} %bitcast.8, bf16[4,16384]{1,0:T(4,128)(2,1)} %vel_any.1, bf16[128,128,128]{2,1,0:T(8,128)(2,1)} %coef_any.1, ...), custom_call_target="tpu_custom_call" | custom-call | flops 67108864 | bytes 16777216 | tf_op jit(solution)/shard_map/field/pallas_call | solution.py:316
  38.5 0.0 copy-done
  38.5 0.0 copy-done.1
  38.5 2.4 %mortar_backward.1 = (f32[4,16384]{1,0:T(4,128)}, bf16[4,1024]{1,0:T(4,128)(2,1)}) custom-call(s32[1,128]{1,0:T(1,128)S(1)} %bitcast.7, s32[1,128]{1,0:T(1,128)S(1)} %bitcast.9, s32[1,1]{1,0:T(1,128)} %bitcast.5.count, bf16[4,1024]{1,0:T(4,128)(2,1)S(1)} %get-tuple-element.7.press, bf16[1024,128]{1,0:T(8,128)(2,1)S(1)} %get-tuple-element.8.full, ...), custom_call_target="tpu_custom_call" | custom-call | flops 33554432 | bytes 4194304 | tf_op jit(solution)/shard_map/mortar_backward/pallas_call | solution.py:364
Async XLA Ops:
  1.3 37.2 %copy-start = (s32[128]{0:T(128)S(1)}, s32[128]{0:T(128)}, u32[]{:S(2)}) copy-start(s32[128]{0:T(128)} %param.8) | copy-start | bytes 1540
  1.3 37.2 %copy-start.1 = (s32[128]{0:T(128)S(1)}, s32[128]{0:T(128)}, u32[]{:S(2)}) copy-start(s32[128]{0:T(128)} %param.9) | copy-start | bytes 1540
